TPU v7x, 32 devices: a whole 2x2x4 slice. The times are simulated.
32 devices in a mesh: ctx: 8 (over z, core), tp: 4 (over y, x).
Axes of the slice: x: 2, y: 2, z: 4, core: 2. Of those that a mesh axis runs over, the one named last changes fastest.
Arguments:
- query_latent: bfloat16 [4096, 64, 512], P('ctx', 'tp'), may hold values from -24 to 24
- query_rope: bfloat16 [4096, 4096], P('ctx', 'tp'), may hold values from -24 to 24
- key_latent: bfloat16 [4096, 512], P('ctx'), may hold values from -6 to 6
- key_rope: bfloat16 [2048, 128], P('ctx'), may hold values from -6 to 6
- block_ids: int32 [16], replicated, may hold values from 0 to 15, as said below
- value_up: bfloat16 [64, 512, 128], P('tp'), may hold values from -0.5 to 0.5
- out_weight: bfloat16 [8192, 7168], P('tp'), may hold values from -0.0625 to 0.0625
- residual: bfloat16 [4096, 7168], P(('ctx', 'tp')), may hold values from -18 to 18
- norm_gain: float32 [7168], replicated, may hold values from 0.1 to 1.9
- gate_weight: bfloat16 [7168, 2048], P('ctx', 'tp'), may hold values from -0.0625 to 0.0625
- up_weight: bfloat16 [7168, 2048], P('ctx', 'tp'), may hold values from -0.0625 to 0.0625
- down_weight: bfloat16 [7168, 2048], P('ctx', 'tp'), may hold values from -0.125 to 0.125
Outputs:
- layer_out: bfloat16 [4096, 7168], P(('ctx', 'tp'))
Inputs may be any that keep to these rules, and one draw needn't show every extreme that they name: `block_ids`: index c of ctx stores blocks 2c and 2c + 1; their two entries sum to 15, and every value appears once.
All inputs are finite; a program needn't handle non-finite values.
Results may differ from a plain program's by a relative error of at most 0.018.
Values may be sent and summed in bfloat16 or wider, within the bound.
A program may use at most 192 MiB of HBM per device.

v0:
```python
import jax
import jax.numpy as jnp
from jax import lax
from jax.sharding import PartitionSpec as P


def from_behind(x, axis, by):
    length = lax.axis_size(axis)
    return lax.ppermute(x, axis, [(i, (i + by) % length) for i in range(length)])


def rms_norm(activation, gain_vector):
    mean_square = jnp.mean(activation * activation, axis=-1, keepdims=True)
    return (activation * lax.rsqrt(mean_square + 1e-06) * gain_vector).astype(jnp.bfloat16)


def local(
    query_latent,
    query_rope,
    key_latent,
    key_rope,
    block_ids,
    value_up,
    out_weight,
    residual,
    norm_gain,
    gate_weight,
    up_weight,
    down_weight,
):
    seq_rows = key_latent.shape[0]
    half_len = seq_rows // 2
    head_count = query_latent.shape[1]
    rope_dim = key_rope.shape[1] // 2
    head_dim = value_up.shape[2]
    ctx_count = lax.axis_size("ctx")
    tp_count = lax.axis_size("tp")
    score_scale = (head_dim + rope_dim) ** (-0.5)
    recv_latent, recv_rope = from_behind((key_latent, key_rope), "ctx", 1)
    keys_lat = jnp.concatenate([key_latent, recv_latent], axis=0)
    keys_rot = jnp.concatenate(
        [key_rope.reshape(seq_rows, rope_dim), recv_rope.reshape(seq_rows, rope_dim)], axis=0
    )
    current = lax.axis_index("ctx")
    previous = (current + ctx_count - 1) % ctx_count
    own_ids = lax.dynamic_slice_in_dim(block_ids, current * 2, 2, 0)
    prev_ids = lax.dynamic_slice_in_dim(block_ids, previous * 2, 2, 0)
    row_index = jnp.arange(seq_rows, dtype=jnp.int32)
    first_half = row_index < half_len
    offset = row_index % half_len
    query_pos = jnp.where(first_half, own_ids[0], own_ids[1]) * half_len + offset
    key_pos = jnp.concatenate(
        [query_pos, jnp.where(first_half, prev_ids[0], prev_ids[1]) * half_len + offset], axis=0
    )
    rope_queries = query_rope.reshape(seq_rows, head_count, rope_dim)
    block_rows = min(seq_rows, 512)

    def attend(block_index):
        scores = jnp.einsum(
            "shl,kl->hsk", query_latent, keys_lat, preferred_element_type=jnp.float32
        )
        scores = scores + jnp.einsum(
            "shr,kr->hsk", rope_queries, keys_rot, preferred_element_type=jnp.float32
        )
        scores = scores * score_scale
        visible = key_pos[None, :] <= query_pos[:, None]
        scores = jnp.where(visible[None], scores, -jnp.inf)
        highest = jnp.max(scores, axis=-1, keepdims=True)
        exponent = jnp.exp(scores - highest)
        weights = (exponent / jnp.sum(exponent, axis=-1, keepdims=True)).astype(jnp.bfloat16)
        blended = jnp.einsum(
            "hsk,kl->shl", weights, keys_lat, preferred_element_type=jnp.float32
        ).astype(jnp.bfloat16)
        values = jnp.einsum(
            "shl,hlv->shv", blended, value_up, preferred_element_type=jnp.float32
        ).astype(jnp.bfloat16)
        return values.reshape(block_rows, head_count * head_dim)

    head_out = lax.map(attend, jnp.arange(seq_rows // block_rows, dtype=jnp.int32)).reshape(
        seq_rows, head_count * head_dim
    )
    share_rows = seq_rows // tp_count
    tp_index = lax.axis_index("tp")
    partial_attn = jnp.dot(head_out, out_weight, preferred_element_type=jnp.float32)
    attn_total = lax.psum(partial_attn.astype(jnp.bfloat16), "tp").astype(jnp.float32)
    all_residual = lax.all_gather(residual, "tp", axis=0, tiled=True)
    hidden_state = all_residual.astype(jnp.float32) + attn_total
    normed_all = rms_norm(hidden_state, norm_gain)
    own_state = lax.dynamic_slice_in_dim(hidden_state, tp_index * share_rows, share_rows, 0)
    gate_full, up_full, down_full = (
        lax.all_gather(gate_weight, "ctx", axis=0, tiled=True),
        lax.all_gather(up_weight, "ctx", axis=0, tiled=True),
        lax.all_gather(down_weight, "ctx", axis=0, tiled=True),
    )
    gate_proj = jnp.dot(normed_all, gate_full, preferred_element_type=jnp.float32)
    up_proj = jnp.dot(normed_all, up_full, preferred_element_type=jnp.float32)
    hidden_units = (jax.nn.silu(gate_proj) * up_proj).astype(jnp.bfloat16)
    shared_part = lax.psum_scatter(
        lax.dot_general(
            hidden_units, down_full, (((1,), (1,)), ((), ())), preferred_element_type=jnp.float32
        ).astype(jnp.bfloat16),
        "tp",
        scatter_dimension=0,
        tiled=True,
    ).astype(jnp.float32)
    return (own_state + shared_part).astype(jnp.bfloat16)


def solution(mesh):
    placed = (
        P("ctx", "tp", None),
        P("ctx", "tp"),
        P("ctx", None),
        P("ctx", None),
        P(),
        P("tp", None, None),
        P("tp", None),
        P(("ctx", "tp"), None),
        P(),
        P("ctx", "tp"),
        P("ctx", "tp"),
        P("ctx", "tp"),
    )
    return jax.shard_map(
        local, mesh=mesh, in_specs=placed, out_specs=P(("ctx", "tp"), None), check_vma=False
    )
```

profile of v0, /device:TPU:0, one launch (start us, length us, event | category | flops | bytes accessed | tf_op | source)
XLA Modules:
  0.0 672.1 jit_solution(7638917272089841626)
XLA Ops:
  7.0 2.7 collective-permute-start.1
  9.7 0.8 fusion.35
  11.1 1.2 fusion.22
  12.3 1.3 multiply_add_fusion
  13.6 1.2 broadcast_compare_fusion
  14.8 0.9 reshape.69
  15.7 1.5 copy.19
  17.3 1.5 collective-permute-done.1
  19.0 18.1 %fusion.3 = f32[1024,512,16]{1,0,2:T(8,128)} fusion(bf16[512,16,512]{2,1,0:T(8,128)(2,1)} %param.12, bf16[512,512]{1,0:T(8,128)(2,1)} %collective-permute-done, bf16[512,512]{1,0:T(8,128)(2,1)} %param.14), kind=kOutput, calls=%fused_computation.11 | convolution fusion | flops 8592031744 | bytes 42991616 | tf_op jit(solution)/shard_map/while/body/eval_jaxpr/shl,kl->hsk/dot_general | solution.py:59
  37.1 24.3 %fusion.37 = (f32[16,512]{1,0:T(8,128)S(1)}, f32[16,512,1024]{1,2,0:T(8,128)}) fusion(f32[1024,512,16]{1,0,2:T(8,128)} %fusion.3, pred[512,1024]{0,1:T(8,128)(4,1)} %broadcast_compare_fusion, bf16[512,16,64]{0,2,1:T(8,128)(2,1)S(1)} %bitcast.36, bf16[512,64]{0,1:T(8,128)(2,1)S(1)} %copy.18, bf16[512,64]{0,1:T(8,128)(2,1)S(1)} %copy.17), kind=kOutput, calls=%fused_computation.51 | convolution fusion | flops 1115948032 | bytes 68845568 | tf_op jit(solution)/shard_map/while/body/eval_jaxpr/sub | solution.py:69
  61.3 17.5 %fusion.9 = bf16[16,512,128]{1,2,0:T(8,128)(2,1)} fusion(bf16[16,512,128]{2,1,0:T(8,128)(2,1)S(1)} %copy-done, f32[16,512,1024]{1,2,0:T(8,128)} %get-tuple-element.41, f32[16,512]{1,0:T(8,128)S(1)} %get-tuple-element.40, bf16[512,512]{1,0:T(8,128)(2,1)} %collective-permute-done, bf16[512,512]{1,0:T(8,128)(2,1)} %param.14), kind=kOutput, calls=%fused_computation.17 | convolution fusion | flops 9687793664 | bytes 38830080 | tf_op jit(solution)/shard_map/while/body/eval_jaxpr/shl,hlv->shv/dot_general | solution.py:74
  78.9 23.3 %convolution_convert_fusion.1 = bf16[512,7168]{1,0:T(8,128)(2,1)} fusion(bf16[512,2048]{0,1:T(8,128)(2,1)} %bitcast.37, bf16[2048,7168]{1,0:T(8,128)(2,1)} %param.18), kind=kOutput, calls=%fused_computation.10 | convolution fusion | flops 15036055552 | bytes 38797312 | tf_op jit(solution)/shard_map/dot_general | solution.py:84
  102.3 0.7 all-gather.5.cloned.1.call-update
  103.0 0.7 all-gather.7.cloned.1.call-update
  104.9 153.2 %all-reduce.2.cloned.1.call-done = bf16[512,7168]{1,0:T(8,128)(2,1)} async-done(((bf16[512,7168]{1,0:T(8,128)(2,1)}), bf16[512,7168]{1,0:T(8,128)(2,1)}) %all-reduce.2.cloned.1.call-update) | async-done | bytes 7340048 | tf_op jit(solution)/shard_map/psum | solution.py:85
  258.1 80.8 %all-gather.5.cloned.1.call-done = bf16[512,7168]{1,0:T(8,128)(2,1)} async-done(((bf16[128,7168]{1,0:T(8,128)(2,1)}), bf16[512,7168]{1,0:T(8,128)(2,1)}) %all-gather.5.cloned.1.call-update) | async-done | bytes 7340048 | tf_op jit(solution)/shard_map/all_gather | solution.py:86
  338.9 13.5 %convert_add_fusion = (f32[512,7168]{1,0:T(8,128)}, f32[512]{0:T(512)S(1)}) fusion(bf16[512,7168]{1,0:T(8,128)(2,1)} %all-reduce.2.cloned.1.call-done, bf16[512,7168]{1,0:T(8,128)(2,1)} %all-gather.5.cloned.1.call-done), kind=kLoop, calls=%fused_computation.7 | loop fusion | flops 18349568 | bytes 29362176 | tf_op jit(solution)/shard_map/add | solution.py:87
  352.4 61.6 %all-gather.7.cloned.1.call-done = bf16[7168,512]{1,0:T(8,128)(2,1)} async-done(((bf16[896,512]{1,0:T(8,128)(2,1)}), bf16[7168,512]{1,0:T(8,128)(2,1)}) %all-gather.7.cloned.1.call-update) | async-done | bytes 7340048 | tf_op jit(solution)/shard_map/all_gather | solution.py:91
  413.9 9.7 %fusion.33 = f32[512,512]{1,0:T(8,128)S(1)} fusion(bf16[7168,512]{1,0:T(8,128)(2,1)} %all-gather.7.cloned.1.call-done, f32[7168]{0:T(1024)S(1)} %copy-done.2, f32[512]{0:T(512)S(1)} %add_rsqrt_fusion, bf16[512,7168]{1,0:T(8,128)(2,1)} %all-reduce.2.cloned.1.call-done, bf16[512,7168]{1,0:T(8,128)(2,1)} %all-gather.5.cloned.1.call-done), kind=kOutput, calls=%fused_computation.47 | convolution fusion | flops 3780116480 | bytes 23099392 | tf_op jit(solution)/shard_map/dot_general | solution.py:95
  423.7 63.8 %all-gather.11.cloned.1.call-done = bf16[7168,512]{1,0:T(8,128)(2,1)} async-done(((bf16[896,512]{1,0:T(8,128)(2,1)}), bf16[7168,512]{1,0:T(8,128)(2,1)}) %all-gather.11.cloned.1.call-update) | async-done | bytes 7340048 | tf_op jit(solution)/shard_map/all_gather | solution.py:93
  487.5 73.5 %all-gather.9.cloned.1.call-done = bf16[7168,512]{1,0:T(8,128)(2,1)} async-done(((bf16[896,512]{1,0:T(8,128)(2,1)}), bf16[7168,512]{1,0:T(8,128)(2,1)}) %all-gather.9.cloned.1.call-update) | async-done | bytes 7340048 | tf_op jit(solution)/shard_map/all_gather | solution.py:92
  561.0 22.3 %convolution_convert_fusion = bf16[512,7168]{1,0:T(8,128)(2,1)} fusion(bf16[7168,512]{1,0:T(8,128)(2,1)} %all-gather.11.cloned.1.call-done, bf16[7168,512]{1,0:T(8,128)(2,1)} %all-gather.9.cloned.1.call-done, f32[512,512]{1,0:T(8,128)S(1)} %fusion.33, f32[7168]{0:T(1024)S(1)} %copy-done.2, f32[512]{0:T(512)S(1)} %add_rsqrt_fusion, ...), kind=kOutput, calls=%fused_computation.9 | convolution fusion | flops 7543455744 | bytes 37779456 | tf_op jit(solution)/shard_map/dot_general | solution.py:99
  583.3 77.7 %reduce-scatter.2.cloned.1.call-done = bf16[128,7168]{1,0:T(8,128)(2,1)} async-done(((bf16[512,7168]{1,0:T(8,128)(2,1)}), bf16[128,7168]{1,0:T(8,128)(2,1)}) %reduce-scatter.2.cloned.1.call-update) | async-done | bytes 1835024 | tf_op jit(solution)/shard_map/reduce_scatter | solution.py:98
  661.1 4.2 add_convert_fusion
  (24 shorter events, 2.7 us)
Async XLA Ops:
  6.5 54.8 %copy-start = (bf16[16,512,128]{2,1,0:T(8,128)(2,1)S(1)}, bf16[16,512,128]{2,1,0:T(8,128)(2,1)}, u32[]{:S(2)}) copy-start(bf16[16,512,128]{2,1,0:T(8,128)(2,1)} %param.17) | copy-start | bytes 6291460
  6.5 251.6 %all-reduce.2.cloned.1.call-start = ((), (), s32[]{:S(2)}) async-start(), calls=%async_computation.2 | async-start | bytes 14680064 | tf_op jit(solution)/shard_map/psum | solution.py:85
  6.5 12.5 %collective-permute-start = (bf16[512,512]{1,0:T(8,128)(2,1)}, bf16[512,512]{1,0:T(8,128)(2,1)}, u32[]{:S(2)}, u32[]{:S(2)}) collective-permute-start(bf16[512,512]{1,0:T(8,128)(2,1)} %param.14), channel_id=1, source_target_pairs={{0,4},{4,8},{8,12},{12,16},{16,20},{20,24},{24,28},{28,0},{1,5},{5... | collective-permute-start | bytes 1572872 | tf_op jit(solution)/shard_map/ppermute | solution.py:9
  7.0 11.8 %collective-permute-start.1 = (bf16[256,128]{1,0:T(8,128)(2,1)}, bf16[256,128]{1,0:T(8,128)(2,1)S(1)}, u32[]{:S(2)}, u32[]{:S(2)}) collective-permute-start(bf16[256,128]{1,0:T(8,128)(2,1)} %param.15), channel_id=1, source_target_pairs={{0,4},{4,8},{8,12},{12,16},{16,20},{20,24},{24,28},{28,0},{1,5},{5... | collective-permute-start | bytes 196616 | tf_op jit(solution)/shard_map/ppermute | solution.py:9
  102.2 236.6 %all-gather.5.cloned.1.call-start = ((), (), s32[]{:S(2)}) async-start(), calls=%async_computation.1 | async-start | bytes 9175040 | tf_op jit(solution)/shard_map/all_gather | solution.py:86
  103.0 311.0 %all-gather.7.cloned.1.call-start = ((), (), s32[]{:S(2)}) async-start(), calls=%async_computation.3 | async-start | bytes 8257536 | tf_op jit(solution)/shard_map/all_gather | solution.py:91
  103.7 383.8 %all-gather.11.cloned.1.call-start = ((), (), s32[]{:S(2)}) async-start(), calls=%async_computation.5 | async-start | bytes 8257536 | tf_op jit(solution)/shard_map/all_gather | solution.py:93
  104.3 456.7 %all-gather.9.cloned.1.call-start = ((), (), s32[]{:S(2)}) async-start(), calls=%async_computation.4 | async-start | bytes 8257536 | tf_op jit(solution)/shard_map/all_gather | solution.py:92
  104.9 309.1 %copy-start.2 = (f32[7168]{0:T(1024)S(1)}, f32[7168]{0:T(1024)}, u32[]{:S(2)}) copy-start(f32[7168]{0:T(1024)} %param.20) | copy-start | bytes 86020
  104.9 556.2 %reduce-scatter.2.cloned.1.call-start = ((), (), s32[]{:S(2)}) async-start(), calls=%async_computation.6 | async-start | bytes 9175040 | tf_op jit(solution)/shard_map/reduce_scatter | solution.py:98
  583.3 81.9 %copy-start.1 = (bf16[16,512,128]{2,1,0:T(8,128)(2,1)S(1)}, bf16[16,512,128]{2,1,0:T(8,128)(2,1)}, u32[]{:S(2)}) copy-start(bf16[16,512,128]{2,1,0:T(8,128)(2,1)} %param.17) | copy-start | bytes 6291460
Sparse Core Ops, SparseCore 0:
  102.3 155.7 all-reduce.1
  259.9 78.8 all-gather.4
  340.5 73.3 all-gather.6
  415.4 71.9 all-gather.10
  489.0 71.9 all-gather.8
  583.5 77.5 reduce-scatter.1
where the time goes:
time: 672 us
  waiting for transfers between devices  515 us (77%)
  matrix products  115 us (17%)
  other arithmetic  21.3 us (3%)
  between operations  13.6 us (2%)
    psum x1, waiting for transfers between devices, local(): lax.psum(partial_attn.astype(jnp.bfloat16), 'tp').astype(jnp.float32)  153 us
    all_gather x1, waiting for transfers between devices, local(): all_residual = lax.all_gather(residual, 'tp', axis=0, tiled=True)  80.8 us
    reduce_scatter x1, waiting for transfers between devices, local(): lax.psum_scatter(lax.dot_general(hidden_units, down_full, (((1,), (1,)),...  77.7 us
    all_gather x1, waiting for transfers between devices, local(): lax.all_gather(up_weight, 'ctx', axis=0, tiled=True)  73.5 us
    all_gather x1, waiting for transfers between devices, local(): lax.all_gather(down_weight, 'ctx', axis=0, tiled=True)  63.8 us
    all_gather x1, waiting for transfers between devices, local(): lax.all_gather(gate_weight, 'ctx', axis=0, tiled=True)  61.6 us
    sub x1, matrix products, attend(): exponent = jnp.exp(scores - highest)  24.3 us
    dot_general x1, matrix products, local(): jnp.dot(head_out, out_weight, preferred_element_type=jnp.float32)  23.3 us
  transfers between devices with their start and end apart: 8, of which 7 were waited for; matrix products, arithmetic and copies ran while one was open for 5% of the time, Pallas kernels for 0%

commit v1 on v0

--- a/solution.py
+++ b/solution.py
@@ -82,7 +82,9 @@
     share_rows = seq_rows // tp_count
     tp_index = lax.axis_index("tp")
     partial_attn = jnp.dot(head_out, out_weight, preferred_element_type=jnp.float32)
-    attn_total = lax.psum(partial_attn.astype(jnp.bfloat16), "tp").astype(jnp.float32)
+    attn_total = jnp.sum(lax.all_gather(partial_attn.astype(jnp.bfloat16), "tp"), axis=0).astype(
+        jnp.float32
+    )
     all_residual = lax.all_gather(residual, "tp", axis=0, tiled=True)
     hidden_state = all_residual.astype(jnp.float32) + attn_total
     normed_all = rms_norm(hidden_state, norm_gain)

time: 672 us -> 779 us (1.16)
  waiting for transfers between devices: 515 us -> 605 us
  other arithmetic: 21.3 us -> 37.5 us
    all_gather x0 -> x1, waiting for transfers between devices: none -> 260 us  [local(): lax.all_gather(partial_attn.astype(jnp.bfloat16), 'tp')]
    psum x1 -> x0, waiting for transfers between devices: 153 us -> none  [local(): lax.psum(partial_attn.astype(jnp.bfloat16), 'tp').astype(jnp.float32)]
    all_gather x1, waiting for transfers between devices: 80.8 us -> 64.6 us  [local(): all_residual = lax.all_gather(residual, 'tp', axis=0, tiled=True)]
    reduce_sum x0 -> x1, other arithmetic: none -> 16.2 us  [local(): jnp.sum(lax.all_gather(partial_attn.astype(jnp.bfloat16), 'tp'), axis=0)]
    all_gather x1, waiting for transfers between devices: 63.8 us -> 73.5 us  [local(): lax.all_gather(down_weight, 'ctx', axis=0, tiled=True)]
    all_gather x1, waiting for transfers between devices: 73.5 us -> 63.8 us  [local(): lax.all_gather(up_weight, 'ctx', axis=0, tiled=True)]
  transfers between devices with their start and end apart: 8 -> 8, of which waited for: 7 -> 7; matrix products, arithmetic and copies ran while one was open for 5% -> 6% of each run, Pallas kernels for 0% -> 0%
where the time goes in v1:
time: 779 us
  waiting for transfers between devices  605 us (78%)
  matrix products  115 us (15%)
  other arithmetic  37.5 us (5%)
  between operations  13.6 us (2%)
    all_gather x1, waiting for transfers between devices, local(): lax.all_gather(partial_attn.astype(jnp.bfloat16), 'tp')  260 us
    reduce_scatter x1, waiting for transfers between devices, local(): lax.psum_scatter(lax.dot_general(hidden_units, down_full, (((1,), (1,)),...  77.8 us
    all_gather x1, waiting for transfers between devices, local(): lax.all_gather(down_weight, 'ctx', axis=0, tiled=True)  73.5 us
    all_gather x1, waiting for transfers between devices, local(): all_residual = lax.all_gather(residual, 'tp', axis=0, tiled=True)  64.6 us
    all_gather x1, waiting for transfers between devices, local(): lax.all_gather(up_weight, 'ctx', axis=0, tiled=True)  63.8 us
    all_gather x1, waiting for transfers between devices, local(): lax.all_gather(gate_weight, 'ctx', axis=0, tiled=True)  61.6 us
    sub x1, matrix products, attend(): exponent = jnp.exp(scores - highest)  24.3 us
    dot_general x1, matrix products, local(): jnp.dot(head_out, out_weight, preferred_element_type=jnp.float32)  23.3 us
  transfers between devices with their start and end apart: 8, of which 7 were waited for; matrix products, arithmetic and copies ran while one was open for 6% of the time, Pallas kernels for 0%

profile of v1, /device:TPU:0, one launch (start us, length us, event | category | flops | bytes accessed | tf_op | source)
XLA Modules:
  0.0 778.6 jit_solution(14536248824211629392)
XLA Ops:
  7.0 2.7 collective-permute-start.1
  9.7 0.8 fusion.35
  11.1 1.2 fusion.22
  12.3 1.3 multiply_add_fusion
  13.6 1.2 broadcast_compare_fusion
  14.8 0.9 reshape.69
  15.7 1.5 copy.19
  17.3 1.5 collective-permute-done.1
  19.0 18.1 %fusion.3 = f32[1024,512,16]{1,0,2:T(8,128)} fusion(bf16[512,16,512]{2,1,0:T(8,128)(2,1)} %param.12, bf16[512,512]{1,0:T(8,128)(2,1)} %collective-permute-done, bf16[512,512]{1,0:T(8,128)(2,1)} %param.14), kind=kOutput, calls=%fused_computation.11 | convolution fusion | flops 8592031744 | bytes 42991616 | tf_op jit(solution)/shard_map/while/body/eval_jaxpr/shl,kl->hsk/dot_general | solution.py:59
  37.1 24.3 %fusion.37 = (f32[16,512]{1,0:T(8,128)S(1)}, f32[16,512,1024]{1,2,0:T(8,128)}) fusion(f32[1024,512,16]{1,0,2:T(8,128)} %fusion.3, pred[512,1024]{0,1:T(8,128)(4,1)} %broadcast_compare_fusion, bf16[512,16,64]{0,2,1:T(8,128)(2,1)S(1)} %bitcast.38, bf16[512,64]{0,1:T(8,128)(2,1)S(1)} %copy.18, bf16[512,64]{0,1:T(8,128)(2,1)S(1)} %copy.17), kind=kOutput, calls=%fused_computation.51 | convolution fusion | flops 1115948032 | bytes 68845568 | tf_op jit(solution)/shard_map/while/body/eval_jaxpr/sub | solution.py:69
  61.3 17.5 %fusion.9 = bf16[16,512,128]{1,2,0:T(8,128)(2,1)} fusion(bf16[16,512,128]{2,1,0:T(8,128)(2,1)S(1)} %copy-done, f32[16,512,1024]{1,2,0:T(8,128)} %get-tuple-element.41, f32[16,512]{1,0:T(8,128)S(1)} %get-tuple-element.40, bf16[512,512]{1,0:T(8,128)(2,1)} %collective-permute-done, bf16[512,512]{1,0:T(8,128)(2,1)} %param.14), kind=kOutput, calls=%fused_computation.17 | convolution fusion | flops 9687793664 | bytes 38830080 | tf_op jit(solution)/shard_map/while/body/eval_jaxpr/shl,hlv->shv/dot_general | solution.py:74
  78.9 23.3 %convolution_convert_fusion.1 = bf16[512,7168]{1,0:T(8,128)(2,1)} fusion(bf16[512,2048]{0,1:T(8,128)(2,1)} %bitcast.39, bf16[2048,7168]{1,0:T(8,128)(2,1)} %param.18), kind=kOutput, calls=%fused_computation.10 | convolution fusion | flops 15036055552 | bytes 38797312 | tf_op jit(solution)/shard_map/dot_general | solution.py:84
  102.3 0.7 all-gather.7.cloned.1.call-update
  104.9 259.7 %all-gather.15.cloned.1.call-done = bf16[2048,7168]{1,0:T(8,128)(2,1)} async-done(((bf16[512,7168]{1,0:T(8,128)(2,1)}), bf16[2048,7168]{1,0:T(8,128)(2,1)}) %all-gather.15.cloned.1.call-update) | async-done | bytes 29360144 | tf_op jit(solution)/shard_map/all_gather | solution.py:85
  364.6 16.2 %reduce_sum.32 = bf16[512,7168]{1,0:T(8,128)(2,1)} reduce(bf16[4,512,7168]{2,1,0:T(8,128)(2,1)} %bitcast.37, bf16[]{:T(256)} %constant.73.clone.1), dimensions={0}, to_apply=%region_2.3 | reduce | flops 11010048 | bytes 36700160 | tf_op jit(solution)/shard_map/reduce_sum | solution.py:85
  380.8 64.6 %all-gather.7.cloned.1.call-done = bf16[512,7168]{1,0:T(8,128)(2,1)} async-done(((bf16[128,7168]{1,0:T(8,128)(2,1)}), bf16[512,7168]{1,0:T(8,128)(2,1)}) %all-gather.7.cloned.1.call-update) | async-done | bytes 7340048 | tf_op jit(solution)/shard_map/all_gather | solution.py:88
  445.4 13.5 %convert_add_fusion = (f32[512,7168]{1,0:T(8,128)}, f32[512]{0:T(512)S(1)}) fusion(bf16[512,7168]{1,0:T(8,128)(2,1)} %reduce_sum.32, bf16[512,7168]{1,0:T(8,128)(2,1)} %all-gather.7.cloned.1.call-done), kind=kLoop, calls=%fused_computation.7 | loop fusion | flops 18349568 | bytes 29362176 | tf_op jit(solution)/shard_map/add | solution.py:89
  458.9 61.6 %all-gather.9.cloned.1.call-done = bf16[7168,512]{1,0:T(8,128)(2,1)} async-done(((bf16[896,512]{1,0:T(8,128)(2,1)}), bf16[7168,512]{1,0:T(8,128)(2,1)}) %all-gather.9.cloned.1.call-update) | async-done | bytes 7340048 | tf_op jit(solution)/shard_map/all_gather | solution.py:93
  520.5 9.7 %fusion.33 = f32[512,512]{1,0:T(8,128)S(1)} fusion(bf16[7168,512]{1,0:T(8,128)(2,1)} %all-gather.9.cloned.1.call-done, f32[7168]{0:T(1024)S(1)} %copy-done.2, f32[512]{0:T(512)S(1)} %add_rsqrt_fusion, bf16[512,7168]{1,0:T(8,128)(2,1)} %reduce_sum.32, bf16[512,7168]{1,0:T(8,128)(2,1)} %all-gather.7.cloned.1.call-done), kind=kOutput, calls=%fused_computation.47 | convolution fusion | flops 3780116480 | bytes 23099392 | tf_op jit(solution)/shard_map/dot_general | solution.py:97
  530.2 63.8 %all-gather.11.cloned.1.call-done = bf16[7168,512]{1,0:T(8,128)(2,1)} async-done(((bf16[896,512]{1,0:T(8,128)(2,1)}), bf16[7168,512]{1,0:T(8,128)(2,1)}) %all-gather.11.cloned.1.call-update) | async-done | bytes 7340048 | tf_op jit(solution)/shard_map/all_gather | solution.py:94
  594.0 73.5 %all-gather.13.cloned.1.call-done = bf16[7168,512]{1,0:T(8,128)(2,1)} async-done(((bf16[896,512]{1,0:T(8,128)(2,1)}), bf16[7168,512]{1,0:T(8,128)(2,1)}) %all-gather.13.cloned.1.call-update) | async-done | bytes 7340048 | tf_op jit(solution)/shard_map/all_gather | solution.py:95
  667.5 22.3 %convolution_convert_fusion = bf16[512,7168]{1,0:T(8,128)(2,1)} fusion(bf16[7168,512]{1,0:T(8,128)(2,1)} %all-gather.13.cloned.1.call-done, bf16[7168,512]{1,0:T(8,128)(2,1)} %all-gather.11.cloned.1.call-done, f32[512,512]{1,0:T(8,128)S(1)} %fusion.33, f32[7168]{0:T(1024)S(1)} %copy-done.2, f32[512]{0:T(512)S(1)} %add_rsqrt_fusion, ...), kind=kOutput, calls=%fused_computation.9 | convolution fusion | flops 7543455744 | bytes 37779456 | tf_op jit(solution)/shard_map/dot_general | solution.py:101
  689.8 77.8 %reduce-scatter.2.cloned.1.call-done = bf16[128,7168]{1,0:T(8,128)(2,1)} async-done(((bf16[512,7168]{1,0:T(8,128)(2,1)}), bf16[128,7168]{1,0:T(8,128)(2,1)}) %reduce-scatter.2.cloned.1.call-update) | async-done | bytes 1835024 | tf_op jit(solution)/shard_map/reduce_scatter | solution.py:100
  767.6 4.2 add_convert_fusion
  (25 shorter events, 3.4 us)
Async XLA Ops:
  6.5 54.8 %copy-start = (bf16[16,512,128]{2,1,0:T(8,128)(2,1)S(1)}, bf16[16,512,128]{2,1,0:T(8,128)(2,1)}, u32[]{:S(2)}) copy-start(bf16[16,512,128]{2,1,0:T(8,128)(2,1)} %param.17) | copy-start | bytes 6291460
  6.5 358.1 %all-gather.15.cloned.1.call-start = ((), (), s32[]{:S(2)}) async-start(), calls=%async_computation.6 | async-start | bytes 36700160 | tf_op jit(solution)/shard_map/all_gather | solution.py:85
  6.5 12.5 %collective-permute-start = (bf16[512,512]{1,0:T(8,128)(2,1)}, bf16[512,512]{1,0:T(8,128)(2,1)}, u32[]{:S(2)}, u32[]{:S(2)}) collective-permute-start(bf16[512,512]{1,0:T(8,128)(2,1)} %param.14), channel_id=1, source_target_pairs={{0,4},{4,8},{8,12},{12,16},{16,20},{20,24},{24,28},{28,0},{1,5},{5... | collective-permute-start | bytes 1572872 | tf_op jit(solution)/shard_map/ppermute | solution.py:9
  7.0 11.8 %collective-permute-start.1 = (bf16[256,128]{1,0:T(8,128)(2,1)}, bf16[256,128]{1,0:T(8,128)(2,1)S(1)}, u32[]{:S(2)}, u32[]{:S(2)}) collective-permute-start(bf16[256,128]{1,0:T(8,128)(2,1)} %param.15), channel_id=1, source_target_pairs={{0,4},{4,8},{8,12},{12,16},{16,20},{20,24},{24,28},{28,0},{1,5},{5... | collective-permute-start | bytes 196616 | tf_op jit(solution)/shard_map/ppermute | solution.py:9
  102.2 343.2 %all-gather.7.cloned.1.call-start = ((), (), s32[]{:S(2)}) async-start(), calls=%async_computation.1 | async-start | bytes 9175040 | tf_op jit(solution)/shard_map/all_gather | solution.py:88
  103.0 417.5 %all-gather.9.cloned.1.call-start = ((), (), s32[]{:S(2)}) async-start(), calls=%async_computation.2 | async-start | bytes 8257536 | tf_op jit(solution)/shard_map/all_gather | solution.py:93
  103.7 490.3 %all-gather.11.cloned.1.call-start = ((), (), s32[]{:S(2)}) async-start(), calls=%async_computation.3 | async-start | bytes 8257536 | tf_op jit(solution)/shard_map/all_gather | solution.py:94
  104.3 563.3 %all-gather.13.cloned.1.call-start = ((), (), s32[]{:S(2)}) async-start(), calls=%async_computation.4 | async-start | bytes 8257536 | tf_op jit(solution)/shard_map/all_gather | solution.py:95
  104.9 662.7 %reduce-scatter.2.cloned.1.call-start = ((), (), s32[]{:S(2)}) async-start(), calls=%async_computation.5 | async-start | bytes 9175040 | tf_op jit(solution)/shard_map/reduce_scatter | solution.py:100
  380.8 139.7 %copy-start.2 = (f32[7168]{0:T(1024)S(1)}, f32[7168]{0:T(1024)}, u32[]{:S(2)}) copy-start(f32[7168]{0:T(1024)} %param.20) | copy-start | bytes 86020
  689.8 82.0 %copy-start.1 = (bf16[16,512,128]{2,1,0:T(8,128)(2,1)S(1)}, bf16[16,512,128]{2,1,0:T(8,128)(2,1)}, u32[]{:S(2)}) copy-start(bf16[16,512,128]{2,1,0:T(8,128)(2,1)} %param.17) | copy-start | bytes 6291460
Sparse Core Ops, SparseCore 0:
  102.3 262.2 all-gather.14
  366.5 78.8 all-gather.6
  447.0 73.3 all-gather.8
  522.0 71.9 all-gather.10
  595.5 71.9 all-gather.12
  690.0 77.5 reduce-scatter.1
